TPU v7x, 128 devices: a whole 4x4x4 slice. The times are simulated.
128 devices in a mesh: sec: 8 (over x, core), op: 16 (over y, z).
Axes of the slice: x: 4, y: 4, z: 4, core: 2. Of those that a mesh axis runs over, the one named last changes fastest.
Arguments:
- psi: bfloat16 [8192, 256], P(('sec', 'op')), may hold values from -6 to 6
- left_env: bfloat16 [384, 32, 256, 256], P('op', 'sec'), may hold values from -0.01953125 to 0.01953125
- right_env: bfloat16 [384, 32, 256, 256], P('op', 'sec'), may hold values from -0.375 to 0.375
- term_src: int32 [384, 32], P('op', 'sec'), may hold values from 0 to 31, as said below
- block_dims: int32 [2, 32], replicated, may hold values from 64 to 256, as said below
Outputs:
- sigma: bfloat16 [8192, 256], P(('sec', 'op'))
Inputs may be any that keep to these rules, and one draw needn't show every extreme that they name: |term_src[t, k] - k| <= 2 for every t and k, and term_src[t, k] = k + 2 for some t and k. `block_dims`: every entry is a multiple of 4; 256 is reached in each row.
All inputs are finite; a program needn't handle non-finite values.
Results may differ from a plain program's by a relative error of at most 0.0049.
Values may be sent and summed in bfloat16 or wider, within the bound.
A program may use at most 128 MiB of HBM per device.

v0:
```python
import jax
import jax.numpy as jnp
from jax import lax
from jax.sharding import PartitionSpec as P


def padded(cells, sides, width):
    for axis, dim in sides:
        count = lax.axis_size(axis)
        ends = count - 1
        head = lax.slice_in_dim(cells, 0, width, axis=dim)
        tail = lax.slice_in_dim(cells, cells.shape[dim] - width, cells.shape[dim], axis=dim)
        cells = jnp.concatenate(
            [
                lax.ppermute(tail, axis, [(i, (i + 1) % count) for i in range(ends)]),
                cells,
                lax.ppermute(head, axis, [((i + 1) % count, i) for i in range(ends)]),
            ],
            axis=dim,
        )
    return cells


def lookup_dims(block_ids, block_dims):
    count = block_dims.shape[1]
    every_id = jnp.arange(count, dtype=jnp.int32)
    match = block_ids[..., None] == every_id
    rows_used = jnp.sum(jnp.where(match, block_dims[0], 0), axis=-1)
    cols_used = jnp.sum(jnp.where(match, block_dims[1], 0), axis=-1)
    return (rows_used, cols_used)


def shards(psi, left_env, right_env, term_src, block_dims):
    side = psi.shape[1]
    per_sec = left_env.shape[1]
    local_rows = psi.shape[0]
    group_size = lax.axis_size("op")
    extended = padded(psi, (("sec", 0),), local_rows)
    gathered = lax.all_gather(extended, "op", axis=0, tiled=True)
    arranged = gathered.reshape(group_size, 3, local_rows, side).transpose(1, 0, 2, 3)
    blocks = arranged.reshape(-1, side, side)
    first_block = lax.axis_index("sec") * per_sec - per_sec
    local_src = term_src - first_block
    selected = jnp.take(blocks, local_src, axis=0)
    places = jnp.arange(side, dtype=jnp.int32)
    rows_used, cols_used = lookup_dims(term_src, block_dims)
    keep = (places[:, None] < rows_used[..., None, None]) & (
        places[None, :] < cols_used[..., None, None]
    )
    masked = jnp.where(keep, selected, jnp.zeros_like(selected))
    half = jnp.einsum(
        "tkij,tkjl->tkil", masked, right_env, preferred_element_type=jnp.float32
    ).astype(jnp.bfloat16)
    partial_value = jnp.einsum("tkij,tkjl->kil", left_env, half, preferred_element_type=jnp.float32)
    partial_value = partial_value.reshape(per_sec * side, side)
    summed = lax.psum_scatter(partial_value, "op", scatter_dimension=0, tiled=True)
    row_start = (lax.axis_index("sec") * group_size + lax.axis_index("op")) * local_rows
    global_rows = row_start + jnp.arange(local_rows, dtype=jnp.int32)
    out_blocks = global_rows // side
    inner_rows = global_rows % side
    out_rows_used, out_cols_used = lookup_dims(out_blocks, block_dims)
    out_keep = (inner_rows < out_rows_used)[:, None] & (places[None, :] < out_cols_used[:, None])
    return jnp.where(out_keep, summed, jnp.zeros_like(summed)).astype(jnp.bfloat16)


def solution(mesh):
    placed = (
        P(("sec", "op"), None),
        P("op", "sec", None, None),
        P("op", "sec", None, None),
        P("op", "sec"),
        P(),
    )
    return jax.shard_map(
        shards, mesh=mesh, in_specs=placed, out_specs=P(("sec", "op"), None), check_vma=False
    )
```

profile of v0, /device:TPU:0, one launch (start us, length us, event | category | flops | bytes accessed | tf_op | source)
XLA Modules:
  0.0 178.6 jit_solution(1798577908962675282)
XLA Ops:
  6.5 0.0 all-gather.2.cloned.1.call-start
  6.5 1.3 collective-permute-start
  7.8 1.3 collective-permute-start.1
  9.1 0.0 collective-permute-done
  9.1 3.8 %collective-permute-done.1 = bf16[64,256]{1,0:T(8,128)(2,1)S(1)} collective-permute-done((bf16[64,256]{1,0:T(8,128)(2,1)}, bf16[64,256]{1,0:T(8,128)(2,1)S(1)}, u32[]{:S(2)}, u32[]{:S(2)}) %collective-permute-start.1) | collective-permute-done | bytes 32800 | tf_op jit(solution)/shard_map/ppermute | solution.py:17
  12.9 1.4 pad_maximum_fusion
  14.3 0.0 all-gather.2.cloned.1.call-update
  14.4 0.0 reduce-scatter.2.cloned.1.call-start
  14.4 0.7 compare_and_fusion
  15.1 0.1 copy.21
  15.2 0.1 reshape.72
  15.3 0.8 slice_bitcast_fusion
  16.1 1.0 select_reduce_fusion.1
  17.0 0.1 iota_compare_fusion
  17.1 45.8 %all-gather.2.cloned.1.call-done = bf16[3072,256]{1,0:T(8,128)(2,1)} async-done(((bf16[192,256]{1,0:T(8,128)(2,1)}), bf16[3072,256]{1,0:T(8,128)(2,1)}) %all-gather.2.cloned.1.call-update) | async-done | bytes 1572880 | tf_op jit(solution)/shard_map/all_gather | solution.py:39
  63.0 1.5 copy.20
  64.5 6.7 %gather_fusion = bf16[96,256,256]{2,1,0:T(8,128)(2,1)} fusion(bf16[12,256,256]{2,1,0:T(8,128)(2,1)S(1)} %bitcast.16, s32[1024]{0:T(1024)S(1)} %pad_clamp_fusion), kind=kCustom, calls=%fused_computation | custom fusion | bytes 25166208 | tf_op jit(solution)/shard_map/jit(_take)/gather | solution.py:44
  71.2 13.9 %fusion.26 = bf16[24,4,256,256]{3,2,0,1:T(8,128)(2,1)} fusion(bf16[24,4,256,256]{3,2,1,0:T(8,128)(2,1)} %param.7, bf16[24,4,256,256]{3,2,1,0:T(8,128)(2,1)} %bitcast.17, pred[24,4]{0,1:T(4,128)(4,1)S(1)} %get-tuple-element.9, pred[24,4,256]{2,0,1:T(8,128)(4,1)S(1)} %get-tuple-element.13, pred[24,4,256]{2,0,1:T(8,128)(4,1)S(1)} %get-tuple-element.14), kind=kOutput, calls=%fused_computation.7.clone.1 | convolution fusion | flops 3246391296 | bytes 37797984 | tf_op jit(solution)/shard_map/tkij,tkjl->tkil/dot_general | solution.py:51
  85.1 12.6 %fusion.1 = f32[4,256,256,1]{1,2,3,0:T(8,128)} fusion(bf16[24,4,256,256]{3,2,1,0:T(8,128)(2,1)} %param.6, bf16[24,4,256,256]{3,2,0,1:T(8,128)(2,1)} %fusion.26), kind=kOutput, calls=%fused_computation.3 | convolution fusion | flops 3221225472 | bytes 26214400 | tf_op jit(solution)/shard_map/tkij,tkjl->kil/dot_general | solution.py:54
  97.7 0.0 reduce-scatter.2.cloned.1.call-update
  97.8 0.1 select_reduce_fusion.3
  97.9 72.4 %reduce-scatter.2.cloned.1.call-done = f32[64,256]{1,0:T(8,128)} async-done(((f32[1024,256]{1,0:T(8,128)}), f32[64,256]{1,0:T(8,128)}) %reduce-scatter.2.cloned.1.call-update) | async-done | bytes 65552 | tf_op jit(solution)/shard_map/reduce_scatter | solution.py:56
  170.2 1.5 select_convert_fusion
  (3 shorter events, 0.0 us)
Async XLA Ops:
  6.5 56.4 %all-gather.2.cloned.1.call-start = ((), (), s32[]{:S(2)}) async-start(), calls=%async_computation.1 | async-start | bytes 1671168 | tf_op jit(solution)/shard_map/all_gather | solution.py:39
  6.5 2.6 %collective-permute-start = (bf16[64,256]{1,0:T(8,128)(2,1)}, bf16[64,256]{1,0:T(8,128)(2,1)S(1)}, u32[]{:S(2)}, u32[]{:S(2)}) collective-permute-start(bf16[64,256]{1,0:T(8,128)(2,1)} %param.5), channel_id=1, source_target_pairs={{0,16},{16,32},{32,48},{48,64},{64,80},{80,96},{96,112},{1,17},{17... | collective-permute-start | bytes 98312 | tf_op jit(solution)/shard_map/ppermute | solution.py:15
  7.8 5.1 %collective-permute-start.1 = (bf16[64,256]{1,0:T(8,128)(2,1)}, bf16[64,256]{1,0:T(8,128)(2,1)S(1)}, u32[]{:S(2)}, u32[]{:S(2)}) collective-permute-start(bf16[64,256]{1,0:T(8,128)(2,1)} %param.5), channel_id=1, source_target_pairs={{16,0},{32,16},{48,32},{64,48},{80,64},{96,80},{112,96},{17,1},{33... | collective-permute-start | bytes 98312 | tf_op jit(solution)/shard_map/ppermute | solution.py:17
  14.4 155.9 %reduce-scatter.2.cloned.1.call-start = ((), (), s32[]{:S(2)}) async-start(), calls=%async_computation.2 | async-start | bytes 1114112 | tf_op jit(solution)/shard_map/reduce_scatter | solution.py:56
Sparse Core Ops, SparseCore 0:
  14.5 48.4 all-gather.1
  97.8 72.3 reduce-scatter.1
where the time goes:
time: 179 us
  waiting for transfers between devices  122 us (68%)
  matrix products  26.5 us (15%)
  between operations  13.5 us (8%)
  local copies, waits for them, and re-layouts  9.16 us (5%)
  other arithmetic  4.82 us (3%)
  starting transfers between devices  2.62 us (1%)
    reduce_scatter x1, waiting for transfers between devices, shards(): lax.psum_scatter(partial_value, 'op', scatter_dimension=0, tiled=True)  72.4 us
    all_gather x1, waiting for transfers between devices, shards(): gathered = lax.all_gather(extended, 'op', axis=0, tiled=True)  45.8 us
    dot_general x1, matrix products, shards(): jnp.einsum('tkij,tkjl->tkil', masked, right_env, preferred_element_type=j...  13.9 us
    dot_general x1, matrix products, shards(): jnp.einsum('tkij,tkjl->kil', left_env, half, preferred_element_type=jnp.f...  12.6 us
    gather x1, local copies, waits for them, and re-layouts, shards(): selected = jnp.take(blocks, local_src, axis=0)  6.71 us
    ppermute x1, waiting for transfers between devices, padded(): lax.ppermute(head, axis, [((i + 1) % count, i) for i in range(ends)])  3.81 us
  transfers between devices with their start and end apart: 4, of which 3 were waited for; matrix products, arithmetic and copies ran while one was open for 2% of the time, Pallas kernels for 0%

commit v1 on v0

--- a/solution.py
+++ b/solution.py
@@ -36,7 +36,8 @@
     local_rows = psi.shape[0]
     group_size = lax.axis_size("op")
     extended = padded(psi, (("sec", 0),), local_rows)
-    gathered = lax.all_gather(extended, "op", axis=0, tiled=True)
+    sent = jnp.stack([extended] * lax.axis_size("op"))
+    gathered = jnp.concatenate(lax.all_to_all(sent, "op", 0, 0), axis=0)
     arranged = gathered.reshape(group_size, 3, local_rows, side).transpose(1, 0, 2, 3)
     blocks = arranged.reshape(-1, side, side)
     first_block = lax.axis_index("sec") * per_sec - per_sec

time: 179 us -> 164 us (0.916)
  waiting for transfers between devices: 122 us -> 100 us
  starting transfers between devices: 2.62 us -> 10.7 us
    all_gather x1 -> x0, waiting for transfers between devices: 45.8 us -> none  [shards(): gathered = lax.all_gather(extended, 'op', axis=0, tiled=True)]
    all_to_all x0 -> x1, waiting for transfers between devices: none -> 19.1 us  [shards(): gathered = jnp.concatenate(lax.all_to_all(sent, 'op', 0, 0), axis=0)]
    all_to_all x0 -> x1, starting transfers between devices: none -> 8.05 us  [shards(): gathered = jnp.concatenate(lax.all_to_all(sent, 'op', 0, 0), axis=0)]
    reduce_scatter x1, waiting for transfers between devices: 72.4 us -> 77.1 us  [shards(): lax.psum_scatter(partial_value, 'op', scatter_dimension=0, tiled=True)]
where the time goes in v1:
time: 164 us
  waiting for transfers between devices  100 us (61%)
  matrix products  26.5 us (16%)
  between operations  13.5 us (8%)
  starting transfers between devices  10.7 us (7%)
  local copies, waits for them, and re-layouts  9.06 us (6%)
  other arithmetic  4.19 us (3%)
    reduce_scatter x1, waiting for transfers between devices, shards(): lax.psum_scatter(partial_value, 'op', scatter_dimension=0, tiled=True)  77.1 us
    all_to_all x1, waiting for transfers between devices, shards(): gathered = jnp.concatenate(lax.all_to_all(sent, 'op', 0, 0), axis=0)  19.1 us
    dot_general x1, matrix products, shards(): jnp.einsum('tkij,tkjl->tkil', masked, right_env, preferred_element_type=j...  13.9 us
    dot_general x1, matrix products, shards(): jnp.einsum('tkij,tkjl->kil', left_env, half, preferred_element_type=jnp.f...  12.6 us
    all_to_all x1, starting transfers between devices, shards(): gathered = jnp.concatenate(lax.all_to_all(sent, 'op', 0, 0), axis=0)  8.05 us
    gather x1, local copies, waits for them, and re-layouts, shards(): selected = jnp.take(blocks, local_src, axis=0)  6.71 us
    ppermute x1, waiting for transfers between devices, padded(): lax.ppermute(head, axis, [((i + 1) % count, i) for i in range(ends)])  3.81 us
  transfers between devices with their start and end apart: 4, of which 3 were waited for; matrix products, arithmetic and copies ran while one was open for 2% of the time, Pallas kernels for 0%

profile of v1, /device:TPU:0, one launch (start us, length us, event | category | flops | bytes accessed | tf_op | source)
XLA Modules:
  0.0 163.9 jit_solution(12191976829752989103)
XLA Ops:
  6.5 1.3 collective-permute-start
  7.8 1.3 collective-permute-start.1
  9.1 0.0 collective-permute-done
  9.1 3.8 %collective-permute-done.1 = bf16[64,256]{1,0:T(8,128)(2,1)S(1)} collective-permute-done((bf16[64,256]{1,0:T(8,128)(2,1)}, bf16[64,256]{1,0:T(8,128)(2,1)S(1)}, u32[]{:S(2)}, u32[]{:S(2)}) %collective-permute-start.1) | collective-permute-done | bytes 32800 | tf_op jit(solution)/shard_map/ppermute | solution.py:17
  12.9 0.8 pad_maximum_fusion
  13.7 1.3 stack.2
  15.0 8.0 %all-to-all-start = ((bf16[16,192,256]{2,1,0:T(8,128)(2,1)}), bf16[16,192,256]{2,1,0:T(8,128)(2,1)S(1)}, u32[]{:S(2)}, u32[]{:S(2)}) async-start(bf16[16,192,256]{2,1,0:T(8,128)(2,1)} %stack.2), calls=%async_computation | async-start | bytes 3145728 | tf_op jit(solution)/shard_map/all_to_all | solution.py:40
  23.1 0.0 reduce-scatter.2.cloned.1.call-start
  23.1 0.7 compare_and_fusion
  23.8 0.1 copy.21
  23.9 0.1 reshape.70
  24.0 0.8 slice_bitcast_fusion
  24.8 1.0 select_reduce_fusion.1
  25.7 0.1 iota_compare_fusion
  25.9 19.1 %all-to-all-done = bf16[16,192,256]{2,1,0:T(8,128)(2,1)S(1)} async-done(((bf16[16,192,256]{2,1,0:T(8,128)(2,1)}), bf16[16,192,256]{2,1,0:T(8,128)(2,1)S(1)}, u32[]{:S(2)}, u32[]{:S(2)}) %all-to-all-start) | async-done | bytes 1572896 | tf_op jit(solution)/shard_map/all_to_all | solution.py:40
  44.9 0.1 copy.20
  45.0 6.7 %gather_fusion = bf16[96,256,256]{2,1,0:T(8,128)(2,1)} fusion(bf16[12,256,256]{2,1,0:T(8,128)(2,1)S(1)} %bitcast.16, s32[1024]{0:T(1024)S(1)} %pad_clamp_fusion), kind=kCustom, calls=%fused_computation | custom fusion | bytes 25166208 | tf_op jit(solution)/shard_map/jit(_take)/gather | solution.py:45
  51.7 13.9 %fusion.26 = bf16[24,4,256,256]{3,2,0,1:T(8,128)(2,1)} fusion(bf16[24,4,256,256]{3,2,1,0:T(8,128)(2,1)} %param.7, bf16[24,4,256,256]{3,2,1,0:T(8,128)(2,1)} %bitcast.17, pred[24,4]{0,1:T(4,128)(4,1)S(1)} %get-tuple-element.9, pred[24,4,256]{2,0,1:T(8,128)(4,1)S(1)} %get-tuple-element.13, pred[24,4,256]{2,0,1:T(8,128)(4,1)S(1)} %get-tuple-element.14), kind=kOutput, calls=%fused_computation.7.clone.1 | convolution fusion | flops 3246391296 | bytes 37797984 | tf_op jit(solution)/shard_map/tkij,tkjl->tkil/dot_general | solution.py:52
  65.6 12.6 %fusion.1 = f32[4,256,256,1]{1,2,3,0:T(8,128)} fusion(bf16[24,4,256,256]{3,2,1,0:T(8,128)(2,1)} %param.6, bf16[24,4,256,256]{3,2,0,1:T(8,128)(2,1)} %fusion.26), kind=kOutput, calls=%fused_computation.3 | convolution fusion | flops 3221225472 | bytes 26214400 | tf_op jit(solution)/shard_map/tkij,tkjl->kil/dot_general | solution.py:55
  78.3 0.0 reduce-scatter.2.cloned.1.call-update
  78.3 0.1 select_reduce_fusion.3
  78.4 77.1 %reduce-scatter.2.cloned.1.call-done = f32[64,256]{1,0:T(8,128)} async-done(((f32[1024,256]{1,0:T(8,128)}), f32[64,256]{1,0:T(8,128)}) %reduce-scatter.2.cloned.1.call-update) | async-done | bytes 65552 | tf_op jit(solution)/shard_map/reduce_scatter | solution.py:57
  155.5 1.5 select_convert_fusion
  (3 shorter events, 0.0 us)
Async XLA Ops:
  6.5 2.6 %collective-permute-start = (bf16[64,256]{1,0:T(8,128)(2,1)}, bf16[64,256]{1,0:T(8,128)(2,1)S(1)}, u32[]{:S(2)}, u32[]{:S(2)}) collective-permute-start(bf16[64,256]{1,0:T(8,128)(2,1)} %param.5), channel_id=1, source_target_pairs={{0,16},{16,32},{32,48},{48,64},{64,80},{80,96},{96,112},{1,17},{17... | collective-permute-start | bytes 98312 | tf_op jit(solution)/shard_map/ppermute | solution.py:15
  7.8 5.1 %collective-permute-start.1 = (bf16[64,256]{1,0:T(8,128)(2,1)}, bf16[64,256]{1,0:T(8,128)(2,1)S(1)}, u32[]{:S(2)}, u32[]{:S(2)}) collective-permute-start(bf16[64,256]{1,0:T(8,128)(2,1)} %param.5), channel_id=1, source_target_pairs={{16,0},{32,16},{48,32},{64,48},{80,64},{96,80},{112,96},{17,1},{33... | collective-permute-start | bytes 98312 | tf_op jit(solution)/shard_map/ppermute | solution.py:17
  15.0 29.9 %all-to-all-start = ((bf16[16,192,256]{2,1,0:T(8,128)(2,1)}), bf16[16,192,256]{2,1,0:T(8,128)(2,1)S(1)}, u32[]{:S(2)}, u32[]{:S(2)}) async-start(bf16[16,192,256]{2,1,0:T(8,128)(2,1)} %stack.2), calls=%async_computation | async-start | bytes 3145728 | tf_op jit(solution)/shard_map/all_to_all | solution.py:40
  23.1 132.4 %reduce-scatter.2.cloned.1.call-start = ((), (), s32[]{:S(2)}) async-start(), calls=%async_computation.2 | async-start | bytes 1114112 | tf_op jit(solution)/shard_map/reduce_scatter | solution.py:57
Sparse Core Ops, SparseCore 0:
  78.4 77.0 reduce-scatter.1
